TPU v7x, 256 devices: a whole 4x4x8 slice. The times are simulated.
256 devices in a mesh: dp: 64 (over y, x, z_hi), tensor: 4 (over z_lo, core).
Axes of the slice: x: 4, y: 4, z: 8 (z_hi: 4, z_lo: 2; z = z_hi * 2 + z_lo), core: 2. Of those that a mesh axis runs over, the one named last changes fastest.
Arguments:
- train_hidden: bfloat16 [512, 128, 14336], P('dp', None, 'tensor')
- train_grads: bfloat16 [512, 128, 4096], P('dp', None, 'tensor'), may hold values from -6 to 6
- train_ids: int32 [512, 128], P('dp'), may hold values from 0 to 128004, as said below
- query_hidden: bfloat16 [16, 1024, 14336], P(None, 'dp', 'tensor')
- query_grads: bfloat16 [16, 1024, 4096], P(None, 'dp', 'tensor'), may hold values from -6 to 6
- query_ids: int32 [16, 1024], P(None, 'dp'), may hold values from 0 to 128004, as said below
- proj_in: bfloat16 [14336, 64], P('tensor'), may hold values from -0.046875 to 0.046875
- proj_out: bfloat16 [4096, 64], P('tensor'), may hold values from -0.09375 to 0.09375
Outputs:
- scores: float32 [16, 512], P(None, ('dp', 'tensor'))
Inputs may be any that keep to these rules, and one draw needn't show every extreme that they name: `train_ids`: id 128004 marks padding and appears only at the end of a sequence; the first 32 tokens of every training sequence are not padding; other ids lie below 128000. `query_ids`: id 128004 marks padding and appears only at the end of a query; the first 256 tokens of every query are not padding; other ids lie below 128000.
All inputs are finite; a program needn't handle non-finite values.
Results may differ from a plain program's by a relative error of at most 0.0003.
Values sent between devices are 32-bit elements; how exact they have to be, the bound alone decides.
A program may use at most 128 MiB of HBM per device.

v0:
```python
import jax
import jax.numpy as jnp
from jax import lax
from jax.sharding import PartitionSpec as P

ITERS = 3


PAD_ID = 128004
DAMP = 0.1


def per_device(
    train_hidden, train_grads, train_ids, query_hidden, query_grads, query_ids, proj_in, proj_out
):
    tensor_size = lax.axis_size("tensor")
    tensor_at = lax.axis_index("tensor")
    seq_local, seq_len, ff_part = train_hidden.shape
    width_part = train_grads.shape[2]
    rank = proj_in.shape[1]
    nquery, qtok, unused_ff = query_hidden.shape
    total_train = seq_local * lax.axis_size("dp")
    seq_share = seq_local // tensor_size
    tok_share = qtok // tensor_size
    side_in = jnp.dot(
        train_hidden.reshape(-1, ff_part), proj_in, preferred_element_type=jnp.float32
    )
    side_out = jnp.dot(
        train_grads.reshape(-1, width_part), proj_out, preferred_element_type=jnp.float32
    )
    train_in = side_in.reshape(seq_local, seq_len, rank)
    train_out = side_out.reshape(seq_local, seq_len, rank)
    side_in = jnp.einsum("qtf,fr->tqr", query_hidden, proj_in, preferred_element_type=jnp.float32)
    side_out = jnp.einsum("qtd,dr->tqr", query_grads, proj_out, preferred_element_type=jnp.float32)
    query_in = side_in
    query_out = side_out
    train_in, train_out, query_in, query_out = (
        lax.psum_scatter(train_in, "tensor", scatter_dimension=0, tiled=True),
        lax.psum_scatter(train_out, "tensor", scatter_dimension=0, tiled=True),
        lax.psum_scatter(query_in, "tensor", scatter_dimension=0, tiled=True),
        lax.psum_scatter(query_out, "tensor", scatter_dimension=0, tiled=True),
    )
    local_ids = lax.dynamic_slice_in_dim(train_ids, tensor_at * seq_share, seq_share, 0)
    mask = (local_ids != PAD_ID).astype(jnp.float32)
    outer = jnp.einsum(
        "sta,stb->sab", train_in * mask[:, :, None], train_out, precision=lax.Precision.HIGHEST
    )
    examples = outer.reshape(seq_share, rank * rank) / jnp.sum(mask, axis=1)[:, None]
    local_ids = lax.dynamic_slice_in_dim(query_ids, tensor_at * tok_share, tok_share, 1)
    mask = (local_ids != PAD_ID).astype(jnp.float32)
    outer = jnp.einsum(
        "tqa,tqb->qab", query_in * mask.T[:, :, None], query_out, precision=lax.Precision.HIGHEST
    )
    partial_value = outer.reshape(nquery, rank * rank)
    counts = jnp.sum(mask, axis=1)
    partial_value, counts, trace = lax.psum(
        (partial_value, counts, jnp.sum(examples * examples)), ("dp", "tensor")
    )
    queries = partial_value / counts[:, None]
    damping = DAMP * (trace / total_train) / (rank * rank)
    solved = jnp.zeros_like(queries)
    residual = queries
    direction = queries
    norm_now = jnp.sum(residual * residual, axis=1)
    for step in range(ITERS):
        inner = jnp.dot(direction, examples.T, precision=lax.Precision.HIGHEST)
        term = jnp.dot(inner, examples, precision=lax.Precision.HIGHEST)
        image = direction + lax.psum(term, ("dp", "tensor")) / (total_train * damping)
        alpha = norm_now / jnp.sum(direction * image, axis=1)
        solved = solved + alpha[:, None] * direction
        residual = residual - alpha[:, None] * image
        fresh = jnp.sum(residual * residual, axis=1)
        direction = residual + (fresh / norm_now)[:, None] * direction
        norm_now = fresh
    return jnp.dot(solved, examples.T, precision=lax.Precision.HIGHEST)


def solution(mesh):
    return jax.shard_map(
        per_device,
        mesh=mesh,
        in_specs=(
            P("dp", None, "tensor"),
            P("dp", None, "tensor"),
            P("dp", None),
            P(None, "dp", "tensor"),
            P(None, "dp", "tensor"),
            P(None, "dp"),
            P("tensor", None),
            P("tensor", None),
        ),
        out_specs=P(None, ("dp", "tensor")),
        check_vma=False,
    )
```

profile of v0, /device:TPU:1, one launch (start us, length us, event | category | flops | bytes accessed | tf_op | source)
XLA Modules:
  0.0 1128.7 jit_solution(6134152055007727880)
XLA Ops:
  6.6 3.5 fusion.2
  11.4 6.1 fusion.6
  17.6 1.5 fusion.16
  20.2 13.8 %reduce-scatter.5.cloned.1.call-done = f32[4,16,64]{2,1,0:T(8,128)} async-done(((f32[16,16,64]{2,1,0:T(8,128)}), f32[4,16,64]{2,1,0:T(8,128)}) %reduce-scatter.5.cloned.1.call-update) | async-done | bytes 16400 | tf_op jit(solution)/shard_map/reduce_scatter | solution.py:40
  34.8 21.6 %reduce-scatter.7.cloned.1.call-done = f32[4,16,64]{2,1,0:T(8,128)} async-done(((f32[16,16,64]{2,1,0:T(8,128)}), f32[4,16,64]{2,1,0:T(8,128)}) %reduce-scatter.7.cloned.1.call-update) | async-done | bytes 16400 | tf_op jit(solution)/shard_map/reduce_scatter | solution.py:41
  56.5 1.8 fusion.24
  59.2 20.1 %reduce-scatter.9.cloned.1.call-done = f32[2,128,64]{1,2,0:T(8,128)} async-done(((f32[8,128,64]{1,2,0:T(8,128)}), f32[2,128,64]{1,2,0:T(8,128)}) %reduce-scatter.9.cloned.1.call-update) | async-done | bytes 65552 | tf_op jit(solution)/shard_map/reduce_scatter | solution.py:38
  79.3 22.8 %reduce-scatter.11.cloned.1.call-done = f32[2,128,64]{1,2,0:T(8,128)} async-done(((f32[8,128,64]{1,2,0:T(8,128)}), f32[2,128,64]{1,2,0:T(8,128)}) %reduce-scatter.11.cloned.1.call-update) | async-done | bytes 65552 | tf_op jit(solution)/shard_map/reduce_scatter | solution.py:39
  102.1 1.7 multiply_reduce_fusion.5
  103.8 77.6 %all-reduce = (f32[16]{0:T(128)S(1)}, f32[]{:T(128)}) all-reduce(f32[16]{0:T(128)S(1)} %get-tuple-element.13, f32[]{:T(128)} %get-tuple-element.17), channel_id=1, replica_groups=mesh['dp'=64,'tensor'=4] {'dp','tensor'}, use_global_device_ids=true, to_apply=%region_4.0 | all-reduce | flops 17 | bytes 136 | tf_op jit(solution)/shard_map/psum | solution.py:56
  181.5 175.0 %all-reduce.6.cloned.1.call-done = f32[16,4096]{1,0:T(8,128)} async-done(((f32[16,4096]{1,0:T(8,128)}), f32[16,4096]{1,0:T(8,128)}) %all-reduce.6.cloned.1.call-update) | async-done | bytes 262160 | tf_op jit(solution)/shard_map/psum | solution.py:56
  356.5 1.5 fusion.33
  358.1 1.1 fusion.32
  359.9 250.9 %all-reduce.8.cloned.1.call-done = f32[16,4096]{1,0:T(8,128)} async-done(((f32[16,4096]{1,0:T(8,128)}), f32[16,4096]{1,0:T(8,128)}) %all-reduce.8.cloned.1.call-update) | async-done | bytes 262160 | tf_op jit(solution)/shard_map/psum | solution.py:68
  610.8 1.2 multiply_reduce_fusion.3
  612.0 1.2 multiply_reduce_fusion.2
  613.8 1.1 fusion.30
  615.0 250.1 %all-reduce.10.cloned.1.call-done = f32[16,4096]{1,0:T(8,128)} async-done(((f32[16,4096]{1,0:T(8,128)}), f32[16,4096]{1,0:T(8,128)}) %all-reduce.10.cloned.1.call-update) | async-done | bytes 262160 | tf_op jit(solution)/shard_map/psum | solution.py:68
  865.2 1.1 multiply_reduce_fusion.1
  866.3 1.2 multiply_reduce_fusion
  868.0 1.1 fusion.29
  869.1 250.4 %all-reduce.12.cloned.1.call-done = f32[16,4096]{1,0:T(8,128)} async-done(((f32[16,4096]{1,0:T(8,128)}), f32[16,4096]{1,0:T(8,128)}) %all-reduce.12.cloned.1.call-update) | async-done | bytes 262160 | tf_op jit(solution)/shard_map/psum | solution.py:68
  1119.6 1.2 fusion.9
  1120.7 1.1 fusion.10
  (44 shorter events, 5.6 us)
Async XLA Ops:
  6.5 11.0 copy-start
  6.5 4.8 copy-start.2
  6.5 3.7 copy-start.3
  6.5 3.7 copy-start.5
  6.5 27.4 %reduce-scatter.5.cloned.1.call-start = ((), (), s32[]{:S(2)}) async-start(), calls=%async_computation.4 | async-start | bytes 163840 | tf_op jit(solution)/shard_map/reduce_scatter | solution.py:40
  10.2 46.3 %reduce-scatter.7.cloned.1.call-start = ((), (), s32[]{:S(2)}) async-start(), calls=%async_computation.5 | async-start | bytes 163840 | tf_op jit(solution)/shard_map/reduce_scatter | solution.py:41
  11.3 68.0 %reduce-scatter.9.cloned.1.call-start = ((), (), s32[]{:S(2)}) async-start(), calls=%async_computation.7 | async-start | bytes 327680 | tf_op jit(solution)/shard_map/reduce_scatter | solution.py:38
  17.5 1.6 copy-start.4
  17.5 84.6 %reduce-scatter.11.cloned.1.call-start = ((), (), s32[]{:S(2)}) async-start(), calls=%async_computation.8 | async-start | bytes 327680 | tf_op jit(solution)/shard_map/reduce_scatter | solution.py:39
  19.1 337.5 %all-reduce.6.cloned.1.call-start = ((), (), s32[]{:S(2)}) async-start(), calls=%async_computation.6 | async-start | bytes 524288 | tf_op jit(solution)/shard_map/psum | solution.py:56
  59.2 551.7 %all-reduce.8.cloned.1.call-start = ((), (), s32[]{:S(2)}) async-start(), calls=%async_computation.9 | async-start | bytes 524288 | tf_op jit(solution)/shard_map/psum | solution.py:68
  356.5 254.3 %copy-start.1 = (f32[16,4096]{1,0:T(8,128)S(1)}, f32[16,4096]{1,0:T(8,128)}, u32[]{:S(2)}) copy-start(f32[16,4096]{1,0:T(8,128)} %all-reduce.6.cloned.1.call-done) | copy-start | bytes 786436
  359.2 505.9 %all-reduce.10.cloned.1.call-start = ((), (), s32[]{:S(2)}) async-start(), calls=%async_computation.10 | async-start | bytes 524288 | tf_op jit(solution)/shard_map/psum | solution.py:68
  615.0 504.6 %all-reduce.12.cloned.1.call-start = ((), (), s32[]{:S(2)}) async-start(), calls=%async_computation.11 | async-start | bytes 524288 | tf_op jit(solution)/shard_map/psum | solution.py:68
Sparse Core Ops, SparseCore 0:
  10.3 23.6 reduce-scatter.4
  36.6 19.7 reduce-scatter.6
  59.0 20.2 reduce-scatter.8
  81.8 20.2 reduce-scatter.10
  107.4 249.0 all-reduce.5
  361.8 248.9 all-reduce.7
  616.3 248.8 all-reduce.9
  870.6 248.8 all-reduce.11
where the time goes:
time: 1130 us
  waiting for transfers between devices  1000 us (88%)
  blocking collectives  77.6 us (7%)
  matrix products  22.7 us (2%)
  between operations  14.2 us (1%)
    psum x3, waiting for transfers between devices, per_device(): lax.psum(term, ('dp', 'tensor')) / (total_train * damping)  751 us
    psum x1, waiting for transfers between devices, per_device(): lax.psum((partial_value, counts, jnp.sum(examples * examples)), ('dp', 't...  175 us
    psum x1, blocking collectives, per_device(): lax.psum((partial_value, counts, jnp.sum(examples * examples)), ('dp', 't...  77.6 us
    reduce_scatter x1, waiting for transfers between devices, per_device(): lax.psum_scatter(train_out, 'tensor', scatter_dimension=0, tiled=True)  22.8 us
  transfers between devices with their start and end apart: 8, of which 8 were waited for; matrix products, arithmetic and copies ran while one was open for 1% of the time, Pallas kernels for 0%

commit v1 on v0

v1 whole, which is shorter than its diff:
```python
import jax
import jax.numpy as jnp
from jax import lax
from jax.experimental import pallas as pl
from jax.experimental.pallas import tpu as pltpu
from jax.sharding import PartitionSpec as P

PAD_ID = 128004
DAMP = 0.1
TRAIN = 512
FEAT = 4096
MESH = pl.DeviceIdType.MESH
F32 = jnp.float32
BF16 = jnp.bfloat16


def kernel(
    th, tg, tids, qh, qg, qids, pin, pout, out,
    TH, TG, QH, QG, PIN, POUT, TIDS, QIDS, WI, WO,
    XQ, XT, RCQ, RCT, YQ, YT, RZQ, RZT,
    QPS, RQ1, CS, RC1, RQ2, ES, EO, EP, EH, EL, RB, SC, FR,
    hsem, cs, cr, zs, zr, q1s, q1r, q2s, q2r, es, er, fs, fr, rs, rr, osem, orem, lsem,
):
    dp = lax.axis_index("dp")
    tt = lax.axis_index("tensor")
    y = lax.div(dp, 16)
    x = lax.rem(lax.div(dp, 4), 4)
    zh = lax.rem(dp, 4)
    zl = lax.div(tt, 2)
    k = lax.rem(tt, 2)
    z = zh * 2 + zl
    col = y * 4 + x
    chip = dp * 2 + zl
    far = 1 - zl
    mate = (dp, zl * 2 + (1 - k))
    across = (dp, far * 2 + k)
    corner = (dp, far * 2 + (1 - k))

    loads = [
        pltpu.make_async_copy(pin, PIN, hsem.at[0]),
        pltpu.make_async_copy(qh, QH, hsem.at[1]),
        pltpu.make_async_copy(pout, POUT, hsem.at[2]),
        pltpu.make_async_copy(qg, QG, hsem.at[3]),
        pltpu.make_async_copy(qids, QIDS, hsem.at[4]),
        pltpu.make_async_copy(tids, TIDS, hsem.at[5]),
    ]
    firsts = []
    for unit in range(4):
        side = far if unit % 2 == 0 else zl
        first = (unit // 2) * 4 + side * 2
        firsts.append(first)
        pair = pl.ds(first, 2)
        loads.append(pltpu.make_async_copy(th.at[pair], TH.at[pair], hsem.at[6 + 2 * unit]))
        loads.append(pltpu.make_async_copy(tg.at[pair], TG.at[pair], hsem.at[7 + 2 * unit]))
    for load in loads:
        load.start()

    def chips(fn):
        def body(n, carry):
            ny = lax.rem(y + lax.rem(lax.div(n, 4), 4), 4)
            nx = lax.rem(x + lax.rem(n, 4), 4)
            nz = lax.rem(z + lax.div(n, 16), 8)
            there = ny * 4 + nx
            fn(there, (there * 4 + lax.div(nz, 2), lax.rem(nz, 2) * 2 + k))
            return carry

        lax.fori_loop(1, 128, body, 0)

    def plane(fn):
        def body(n, carry):
            there = lax.rem(y + lax.div(n, 4), 4) * 4 + lax.rem(x + lax.rem(n, 4), 4)
            fn(there, (there * 4 + zh, tt))
            return carry

        lax.fori_loop(1, 16, body, 0)

    barrier = pltpu.get_barrier_semaphore()

    def greet(there, device):
        pl.semaphore_signal(barrier, inc=1, device_id=device, device_id_type=MESH)

    chips(greet)
    greet(0, mate)
    greet(0, corner)

    def remote(src, dst, send, recv, device):
        return pltpu.make_async_remote_copy(
            src_ref=src, dst_ref=dst, send_sem=send, recv_sem=recv,
            device_id=device, device_id_type=MESH,
        )

    def drain(ref, sem):
        pltpu.make_async_copy(ref, ref, sem).wait()

    def project(hidden, grads):
        return jnp.dot(hidden, WI[...], preferred_element_type=F32) + jnp.dot(
            grads, WO[...], preferred_element_type=F32
        )

    loads[0].wait()
    WI[...] = jnp.concatenate([PIN[...], jnp.zeros_like(PIN)], axis=1)
    loads[2].wait()
    WO[...] = jnp.concatenate([jnp.zeros_like(POUT), POUT[...]], axis=1)

    loads[1].wait()
    loads[3].wait()
    XQ[...] = project(QH[...].reshape(256, -1), QG[...].reshape(256, -1)).reshape(2, 2, 64, 128)
    pl.semaphore_wait(barrier, 129)
    core_q = remote(XQ.at[:, 1 - k], RCQ, cs.at[0], cr.at[0], mate)
    core_q.start()

    def train_unit(unit):
        pair = pl.ds(firsts[unit], 2)
        loads[6 + 2 * unit].wait()
        loads[7 + 2 * unit].wait()
        XT[unit] = project(TH[pair].reshape(256, -1), TG[pair].reshape(256, -1)).reshape(2, 128, 128)
        copy = remote(XT.at[unit, 1 - k], RCT.at[unit], cs.at[1 + unit], cr.at[1 + unit], mate)
        copy.start()
        return copy

    def core_sum(unit, copy):
        copy.wait_recv()
        YT[unit] = XT[unit, k] + RCT[unit]

    def cross(chunk):
        copy = remote(YT.at[2 * chunk], RZT.at[chunk], zs.at[1 + chunk], zr.at[1 + chunk], across)
        copy.start()
        return copy

    lane = lax.broadcasted_iota(jnp.int32, (32, 128), 1)

    def pack(both):
        return jnp.where(lane < 64, pltpu.roll(both[0:32], 64, 1), both[32:64])

    core_0 = train_unit(0)

    core_q.wait_recv()
    YQ[...] = XQ[:, k] + RCQ[...]
    cross_q = remote(YQ.at[far], RZQ, zs.at[0], zr.at[0], across)
    cross_q.start()

    core_1 = train_unit(1)
    core_sum(0, core_0)
    cross_a = cross(0)

    cross_q.wait_recv()
    loads[4].wait()
    side = YQ[zl] + RZQ[...]
    mask = (QIDS[pl.ds(tt * 4, 4), :] != PAD_ID).astype(F32)
    CS[...] = jnp.broadcast_to(jnp.sum(mask, axis=1, keepdims=True), (4, 128))
    wide = jnp.concatenate([mask] * 4, axis=1)
    owner = lax.div(lax.broadcasted_iota(jnp.int32, (4, 64), 1), 16)
    wide = jnp.where(owner == lax.broadcasted_iota(jnp.int32, (4, 64), 0), wide, 0.0)
    turned = side.T[0:64]
    masked = jnp.concatenate([turned * wide[q : q + 1] for q in range(4)], axis=0)
    both = jnp.dot(masked, side, precision=lax.Precision.HIGHEST, preferred_element_type=F32)
    for q in range(4):
        QPS[pl.ds(q, 32, stride=4), :] = pack(both[q * 64 : q * 64 + 64])

    def send_q1(there, device):
        remote(QPS.at[pl.ds(there * 8, 8)], RQ1.at[col], q1s.at[0], q1r.at[0], device).start()
        remote(CS, RC1.at[col], q1s.at[1], q1r.at[1], device).start()

    plane(send_q1)
    own_q = pltpu.make_async_copy(QPS.at[pl.ds(col * 8, 8)], RQ1.at[col], lsem.at[0])
    own_q.start()
    RC1[col] = CS[...]

    core_2 = train_unit(2)
    core_sum(1, core_1)

    def example(chunk, copy):
        copy.wait_recv()
        seq = chunk * 4 + tt
        tokens = YT[2 * chunk + 1] + RZT[chunk]
        mask = (TIDS[pl.ds(seq, 1), :] != PAD_ID).astype(F32)
        both = jnp.dot(
            tokens.T[0:64] * mask, tokens,
            precision=lax.Precision.HIGHEST, preferred_element_type=F32,
        )
        ES[chunk] = pack(both) / jnp.sum(mask, axis=1, keepdims=True)
        spot = pl.ds(chip * 2, 2)

        def send(there, device):
            remote(
                ES.at[chunk, pl.ds(there * 2, 2)], EO.at[chunk, spot], es.at[chunk], er.at[chunk], device
            ).start()

        chips(send)
        own = pltpu.make_async_copy(
            ES.at[chunk, pl.ds(col * 2, 2)], EO.at[chunk, spot], lsem.at[1 + chunk]
        )
        own.start()
        return own

    core_3 = train_unit(3)
    core_sum(2, core_2)
    cross_b = cross(1)
    loads[5].wait()
    own_a = example(0, cross_a)
    core_sum(3, core_3)

    own_q.wait()
    drain(RQ1.at[pl.ds(0, 15)], q1r.at[0])
    drain(RC1.at[pl.ds(0, 15)], q1r.at[1])
    RQ2[zh, 0:8] = jnp.sum(RQ1[...], axis=0)
    RQ2[zh, 8:12] = jnp.sum(RC1[...], axis=0)
    for n in range(1, 4):
        device = (col * 4 + lax.rem(zh + n, 4), tt)
        remote(RQ2.at[zh], RQ2.at[zh], q2s, q2r, device).start()

    own_b = example(1, cross_b)

    def gathered(chunk, own):
        own.wait()
        drain(EO.at[chunk, pl.ds(0, 254)], er.at[chunk])
        copy = remote(EO.at[chunk], EP.at[chunk], fs.at[chunk], fr.at[chunk], mate)
        copy.start()
        return copy

    squares = jnp.zeros((128, 128), F32)

    def halves(ref, chunk, at, squares):
        for f in range(2):
            block = ref[chunk, pl.ds(f, 128, stride=2), :]
            squares = squares + block * block
            high = block.astype(BF16)
            EH[pl.ds(at, 128), f * 128 : f * 128 + 128] = high
            EL[pl.ds(at, 128), f * 128 : f * 128 + 128] = (block - high.astype(F32)).astype(BF16)
        return squares

    fwd_a = gathered(0, own_a)
    drain(RQ2.at[pl.ds(0, 3)], q2r)
    total = jnp.sum(RQ2[...], axis=0)
    queries = jnp.concatenate([total[0:4], total[4:8]], axis=1) / total[8:12, 0:1]
    squares = halves(EO, 0, 0, squares)
    fwd_a.wait_recv()
    squares = halves(EP, 0, 256, squares)
    fwd_b = gathered(1, own_b)
    squares = halves(EO, 1, 128, squares)
    fwd_b.wait_recv()
    squares = halves(EP, 1, 384, squares)

    def stacked(v):
        high = v.astype(BF16).astype(F32)
        return jnp.concatenate([high, v - high], axis=0).astype(BF16)

    def product(v, contract):
        v = stacked(v)
        dims = (((1,), (contract,)), ((), ()))
        whole = lax.dot_general(v, EH[...], dims, preferred_element_type=F32) + lax.dot_general(
            v, EL[...], dims, preferred_element_type=F32
        )
        return whole[0:4] + whole[4:8]

    spot = lax.broadcasted_iota(jnp.int32, (4, 128), 1)

    def share(step, partial_value, first, second):
        for b in range(4):
            RB[step, col, b] = partial_value[:, b * 128 : b * 128 + 128]
        RB[step, col, 4] = jnp.where(spot == 0, first, jnp.where(spot == 1, second, 0.0))

        def send(there, device):
            remote(RB.at[step, col], RB.at[step, col], rs.at[step], rr.at[step], device).start()

        plane(send)
        drain(RB.at[step, pl.ds(0, 15)], rr.at[step])
        whole = jnp.sum(RB[step], axis=0)
        return (
            jnp.concatenate([whole[b] for b in range(4)], axis=1),
            whole[4][:, 0:1],
            whole[4][:, 1:2],
        )

    def rowsum(v):
        return jnp.sum(v, axis=1, keepdims=True)

    residual = direction = queries
    trace = jnp.sum(jnp.sum(squares, axis=0, keepdims=True), axis=1, keepdims=True)
    seen, norm_now, trace = share(0, product(residual, 1), rowsum(residual * residual), trace)
    scale = TRAIN * (DAMP * (trace / TRAIN) / FEAT)
    length = norm_now
    scores = None
    for step in range(3):
        alpha = norm_now / (length + rowsum(seen * seen) / scale)
        scores = alpha * seen if step == 0 else scores + alpha * seen
        if step == 2:
            break
        image = direction + product(seen, 0) / scale
        residual = residual - alpha * image
        fresh_seen, fresh, along = share(
            step + 1, product(residual, 1), rowsum(residual * residual), rowsum(residual * direction)
        )
        beta = fresh / norm_now
        seen = fresh_seen + beta * seen
        length = fresh + 2.0 * beta * along + beta * beta * length
        direction = residual + beta * direction
        norm_now = fresh

    for chunk in range(2):
        for h in range(2):
            b = h * 2 + chunk
            SC[chunk, h] = scores[:, b * 128 : b * 128 + 128]
    for n, (oz, ok, device) in enumerate(((zl, 1 - k, mate), (far, k, across), (far, 1 - k, corner))):
        for p in range(2):
            remote(
                SC.at[oz, lax.rem(p + k, 2)], FR.at[p, tt], osem.at[n], orem.at[n * 2 + p], device
            ).start()
    for p in range(2):
        FR[p, tt] = SC[zl, lax.rem(p + k, 2)]
    for n in range(6):
        drain(FR.at[0, 0], orem.at[n])
    place = lax.broadcasted_iota(jnp.int32, (4, 4, 128), 2) == dp * 2 + k
    left = jnp.sum(jnp.where(place, FR[0], 0.0), axis=2, keepdims=True)
    right = jnp.sum(jnp.where(place, FR[1], 0.0), axis=2, keepdims=True)
    out[...] = jnp.where(lax.broadcasted_iota(jnp.int32, (4, 4, 2), 2) == 0, left, right)

    core_q.wait_send()
    cross_q.wait_send()
    for copy in (core_0, core_1, core_2, core_3, cross_a, cross_b, fwd_a, fwd_b):
        copy.wait_send()
    drain(RQ1.at[pl.ds(0, 15)], q1s.at[0])
    drain(RC1.at[pl.ds(0, 15)], q1s.at[1])
    drain(RQ2.at[pl.ds(0, 3)], q2s)
    for chunk in range(2):
        drain(EO.at[chunk, pl.ds(0, 254)], es.at[chunk])
    for step in range(3):
        drain(RB.at[step, pl.ds(0, 15)], rs.at[step])
    for n in range(3):
        drain(FR.at[0, pl.ds(0, 2)], osem.at[n])


def per_device(th, tg, tids, qh, qg, qids, pin, pout):
    V = pltpu.VMEM
    D = pltpu.SemaphoreType.DMA
    scores = pl.pallas_call(
        kernel,
        out_shape=jax.ShapeDtypeStruct((4, 4, 2), F32),
        in_specs=[pl.BlockSpec(memory_space=pl.ANY)] * 8,
        out_specs=pl.BlockSpec(memory_space=pltpu.VMEM),
        scratch_shapes=[
            V(th.shape, BF16), V(tg.shape, BF16), V(qh.shape, BF16), V(qg.shape, BF16),
            V(pin.shape, BF16), V(pout.shape, BF16), V(tids.shape, jnp.int32), V(qids.shape, jnp.int32),
            V((pin.shape[0], 128), BF16), V((pout.shape[0], 128), BF16),
            V((2, 2, 64, 128), F32), V((4, 2, 128, 128), F32),
            V((2, 64, 128), F32), V((4, 128, 128), F32),
            V((2, 64, 128), F32), V((4, 128, 128), F32),
            V((64, 128), F32), V((2, 128, 128), F32),
            V((128, 128), F32), V((16, 8, 128), F32),
            V((4, 128), F32), V((16, 4, 128), F32),
            V((4, 12, 128), F32),
            V((2, 32, 128), F32), V((2, 256, 128), F32), V((2, 256, 128), F32),
            V((512, 256), BF16), V((512, 256), BF16),
            V((3, 16, 5, 4, 128), F32),
            V((2, 2, 4, 128), F32), V((2, 4, 4, 128), F32),
            D((14,)), D((5,)), D((5,)), D((3,)), D((3,)), D((2,)), D((2,)), D, D,
            D((2,)), D((2,)), D((2,)), D((2,)), D((3,)), D((3,)), D((3,)), D((6,)), D((3,)),
        ],
        compiler_params=pltpu.CompilerParams(
            collective_id=0, has_side_effects=True, vmem_limit_bytes=56 * 1024 * 1024
        ),
        cost_estimate=pl.CostEstimate(flops=10**9, bytes_accessed=13 * 10**6, transcendentals=0),
    )(th, tg, tids, qh, qg, qids, pin, pout)
    return scores.reshape(16, 2)


def solution(mesh):
    return jax.shard_map(
        per_device,
        mesh=mesh,
        in_specs=(
            P("dp", None, "tensor"),
            P("dp", None, "tensor"),
            P("dp", None),
            P(None, "dp", "tensor"),
            P(None, "dp", "tensor"),
            P(None, "dp"),
            P("tensor", None),
            P("tensor", None),
        ),
        out_specs=P(None, ("dp", "tensor")),
        check_vma=False,
    )
```

time: 1130 us -> 63.4 us (0.06)
  waiting for transfers between devices: 1000 us -> 0 us
  blocking collectives: 77.6 us -> 0 us
  Pallas kernels: 0 us -> 57.9 us
  matrix products: 22.7 us -> 0 us
  between operations: 14.2 us -> 0.01 us
    psum x4 -> x0, waiting for transfers between devices: 926 us -> none  [the longest x3 751 us: per_device(): lax.psum(term, ('dp', 'tensor')) / (total_train * damping)]
    reduce_scatter x4 -> x0, waiting for transfers between devices: 78.3 us -> none  [the longest x1 22.8 us: per_device(): lax.psum_scatter(train_out, 'tensor', scatter_dimension=0, tiled=True)]
    psum x1 -> x0, blocking collectives: 77.6 us -> none  [per_device(): lax.psum((partial_value, counts, jnp.sum(examples * examples)), ('dp', 't...]
    pallas_call x0 -> x1, Pallas kernels: none -> 57.9 us  [per_device(): pl.pallas_call(kernel, out_shape=jax.ShapeDtypeStruct((4, 4, 2), F32), in...]
    dot_general x13 -> x0, matrix products: 22.7 us -> none  [the longest x1 6.09 us: per_device(): jnp.dot(train_hidden.reshape(-1, ff_part), proj_in, preferred_element_typ...]
  transfers between devices with their start and end apart: 8 -> 0, of which waited for: 8 -> 0; matrix products, arithmetic and copies ran while one was open for 1% -> 0% of each run, Pallas kernels for 0% -> 0%
where the time goes in v1:
time: 63.4 us; the launch traced here: 63.2 us
  Pallas kernels  57.9 us (91%)
  local copies, waits for them, and re-layouts  5.32 us (8%)
    pallas_call x1, Pallas kernels, per_device(): pl.pallas_call(kernel, out_shape=jax.ShapeDtypeStruct((4, 4, 2), F32), in...  57.9 us
    unnamed x2, local copies, waits for them, and re-layouts  3.99 us
    reshape x1, local copies, waits for them, and re-layouts, per_device(): return scores.reshape(16, 2)  1.33 us

profile of v1, /device:TPU:1, one launch (start us, length us, event | category | flops | bytes accessed | tf_op | source)
XLA Modules:
  0.0 63.2 jit_solution(12479481022484967834)
XLA Ops:
  0.0 1.7 %copy.10.pout = bf16[1024,64]{1,0:T(8,128)(2,1)} copy(bf16[1024,64]{0,1:T(8,128)(2,1)} %param.15) | data formatting | bytes 262144 | tf_op args[7]
  1.7 2.3 %copy.9.pin = bf16[3584,64]{1,0:T(8,128)(2,1)} copy(bf16[3584,64]{0,1:T(8,128)(2,1)} %param.14) | data formatting | bytes 917504 | tf_op args[6]
  4.0 57.9 %shard_map.82 = f32[4,4,2]{2,1,0:T(4,128)} custom-call(bf16[8,128,3584]{2,1,0:T(8,128)(2,1)} %th.1, bf16[8,128,1024]{2,1,0:T(8,128)(2,1)} %tg.1, s32[8,128]{1,0:T(8,128)} %tids.1, bf16[16,16,3584]{2,1,0:T(8,128)(2,1)} %qh.1, bf16[16,16,1024]{2,1,0:T(8,128)(2,1)} %qg.1, s32[16,16]{1,0:T(8,128)} %qids.1, bf16[3584,64]{1,0:T(8,128)(2,1)} %copy.9.pin, ...), custom_call_target="tpu_custom_call" | custom-call | flops 1000000000 | bytes 13000000 | tf_op jit(solution)/shard_map/pallas_call | solution.py:336
  61.9 1.3 %copy.12 = f32[16,2]{0,1:T(2,128)} copy(f32[16,2]{1,0:T(8,128)} %bitcast.1) | data formatting | bytes 256 | tf_op jit(solution)/shard_map/reshape | solution.py:364

commit v2 on v1

v2 whole, which is shorter than its diff:
```python
import jax
import jax.numpy as jnp
from jax import lax
from jax.experimental import pallas as pl
from jax.experimental.pallas import tpu as pltpu
from jax.sharding import PartitionSpec as P

PAD_ID = 128004
DAMP = 0.1
TRAIN = 512
FEAT = 4096
MESH = pl.DeviceIdType.MESH
F32 = jnp.float32
BF16 = jnp.bfloat16


SLOT = (0, 1, 3, 5, 7, 6, 4, 2)


def kernel(
    th, tg, tids, qh, qg, qids, pin, pout, out,
    TH, TG, QH, QG, TIDS, QIDS, WI, WO,
    XQ, XT, RCQ, RCT, YQ, YT, RZQ, RZT,
    QPS, RQ1, CS, RC1, RQ2, ES, EO, EP, EH, EL, RB, SC, FR,
    hsem, cs, cr, zs, zr, q1s, q1r, q2s, q2r, es, er, fs, fr, rs, rr, osem, orem, lsem, inside,
):
    dp = lax.axis_index("dp")
    tt = lax.axis_index("tensor")
    y = lax.div(dp, 16)
    x = lax.rem(lax.div(dp, 4), 4)
    zh = lax.rem(dp, 4)
    zl = lax.div(tt, 2)
    k = lax.rem(tt, 2)
    z = zh * 2 + zl
    col = y * 4 + x
    far = 1 - zl
    mate = (dp, zl * 2 + (1 - k))
    across = (dp, far * 2 + k)
    corner = (dp, far * 2 + (1 - k))

    def column(n):
        m = lax.rem(n + 10, 16)
        return lax.rem(y + lax.div(m, 4), 4) * 4 + lax.rem(x + lax.rem(m, 4), 4)

    def level(there, step):
        nz = lax.rem(z + step, 8)
        return (there * 4 + lax.div(nz, 2), lax.rem(nz, 2) * 2 + k)

    def plane(fn):
        def body(n, carry):
            there = column(n)
            fn(there, (there * 4 + zh, tt))
            return carry

        lax.fori_loop(0, 6, body, 0)
        lax.fori_loop(7, 16, body, 0)

    barrier = pltpu.get_barrier_semaphore()

    def greet(device):
        pl.semaphore_signal(barrier, inc=1, device_id=device, device_id_type=MESH)

    plane(lambda there, device: greet(device))
    for step in range(1, 8):
        greet(level(col, step))
    greet(mate)
    greet(corner)

    loads = [
        pltpu.make_async_copy(pin, WI.at[0:64], hsem.at[0]),
        pltpu.make_async_copy(qh, QH, hsem.at[1]),
        pltpu.make_async_copy(pout, WO.at[64:128], hsem.at[2]),
        pltpu.make_async_copy(qg, QG, hsem.at[3]),
        pltpu.make_async_copy(qids, QIDS, hsem.at[4]),
        pltpu.make_async_copy(tids, TIDS, hsem.at[5]),
    ]
    for unit in range(4):
        pair = pl.ds((unit % 2) * 4 + (far if unit < 2 else zl) * 2, 2)
        loads.append(pltpu.make_async_copy(th.at[pair], TH.at[unit], hsem.at[6 + 2 * unit]))
        loads.append(pltpu.make_async_copy(tg.at[pair], TG.at[unit], hsem.at[7 + 2 * unit]))
    for load in loads:
        load.start()

    def remote(src, dst, send, recv, device):
        return pltpu.make_async_remote_copy(
            src_ref=src, dst_ref=dst, send_sem=send, recv_sem=recv,
            device_id=device, device_id_type=MESH,
        )

    def drain(ref, sem):
        pltpu.make_async_copy(ref, ref, sem).wait()

    def project(hidden, grads):
        dims = (((1,), (1,)), ((), ()))
        return lax.dot_general(hidden, WI[...], dims, preferred_element_type=F32) + lax.dot_general(
            grads, WO[...], dims, preferred_element_type=F32
        )

    WI[64:128] = jnp.zeros_like(WI[64:128])
    WO[0:64] = jnp.zeros_like(WO[0:64])
    for n in range(4):
        loads[n].wait()
    for half in range(2):
        rows = slice(half * 8, half * 8 + 8)
        XQ[half] = project(QH[rows].reshape(128, -1), QG[rows].reshape(128, -1)).reshape(2, 64, 128)
    for unit in range(4):
        loads[6 + 2 * unit].wait()
        loads[7 + 2 * unit].wait()
        for half in range(2):
            XT[unit, half] = project(TH[unit, half], TG[unit, half])

    pl.semaphore_wait(barrier, 24)
    core = [remote(XT.at[u, 1 - k], RCT.at[u], cs.at[u], cr.at[u], mate) for u in range(4)]
    core_q = remote(XQ.at[:, 1 - k], RCQ, cs.at[4], cr.at[4], mate)
    for copy in core[:2] + [core_q] + core[2:]:
        copy.start()
    for step in range(1, 8):
        pl.semaphore_signal(inside, inc=1, device_id=level(col, step), device_id_type=MESH)

    cross = []
    for u in range(2):
        core[u].wait_recv()
        YT[u] = XT[u, k] + RCT[u]
        copy = remote(YT.at[u], RZT.at[u], zs.at[u], zr.at[u], across)
        copy.start()
        cross.append(copy)
    core_q.wait_recv()
    YQ[...] = XQ[:, k] + RCQ[...]
    cross_q = remote(YQ.at[far], RZQ, zs.at[2], zr.at[2], across)
    cross_q.start()
    for u in range(2, 4):
        core[u].wait_recv()
        YT[u] = XT[u, k] + RCT[u]

    lane = lax.broadcasted_iota(jnp.int32, (32, 128), 1)

    def pack(both):
        return jnp.where(lane < 64, pltpu.roll(both[0:32], 64, 1), both[32:64])

    def send_features(chunk, there, steps):
        for step in steps:
            slot = SLOT[step]
            remote(
                ES.at[chunk, pl.ds(there * 2, 2)], EO.at[slot, pl.ds(col * 4 + chunk * 2, 2)],
                es.at[slot], er.at[slot], level(there, step),
            ).start()

    loads[5].wait()
    owns = []
    for chunk in range(2):
        cross[chunk].wait_recv()
        tokens = YT[2 + chunk] + RZT[chunk]
        mask = (TIDS[pl.ds(chunk * 4 + tt, 1), :] != PAD_ID).astype(F32)
        both = jnp.dot(
            tokens.T[0:64] * mask, tokens,
            precision=lax.Precision.HIGHEST, preferred_element_type=F32,
        )
        packed = pack(both) / jnp.sum(mask, axis=1, keepdims=True)
        for f in range(2):
            ES[chunk, pl.ds(f, 16, stride=2), :] = packed[f * 16 : f * 16 + 16]
        if chunk == 0:
            pl.semaphore_wait(inside, 7)

        def features(n, carry, chunk=chunk):
            send_features(chunk, column(n), (4, 5, 3, 6, 2, 7, 1, 0))
            return carry

        lax.fori_loop(0, 6, features, 0)
        lax.fori_loop(7, 16, features, 0)
        send_features(chunk, col, (4, 5, 3, 6, 2, 7, 1))
        own = pltpu.make_async_copy(
            ES.at[chunk, pl.ds(col * 2, 2)], EO.at[0, pl.ds(col * 4 + chunk * 2, 2)], lsem.at[1 + chunk]
        )
        own.start()
        owns.append(own)

    loads[4].wait()
    cross_q.wait_recv()
    side = YQ[zl] + RZQ[...]
    mask = (QIDS[pl.ds(tt * 4, 4), :] != PAD_ID).astype(F32)
    CS[...] = jnp.broadcast_to(jnp.sum(mask, axis=1, keepdims=True), (4, 128))
    wide = jnp.concatenate([mask] * 4, axis=1)
    owner = lax.div(lax.broadcasted_iota(jnp.int32, (4, 64), 1), 16)
    wide = jnp.where(owner == lax.broadcasted_iota(jnp.int32, (4, 64), 0), wide, 0.0)
    turned = side.T[0:64]
    masked = jnp.concatenate([turned * wide[q : q + 1] for q in range(4)], axis=0)
    both = jnp.dot(masked, side, precision=lax.Precision.HIGHEST, preferred_element_type=F32)
    for q in range(4):
        packed = pack(both[q * 64 : q * 64 + 64])
        for f in range(2):
            QPS[pl.ds(f * 4 + q, 16, stride=8), :] = packed[f * 16 : f * 16 + 16]

    def send_q1(there, device):
        remote(QPS.at[pl.ds(there * 8, 8)], RQ1.at[col], q1s.at[0], q1r.at[0], device).start()
        remote(CS, RC1.at[col], q1s.at[1], q1r.at[1], device).start()

    plane(send_q1)
    own_q = pltpu.make_async_copy(QPS.at[pl.ds(col * 8, 8)], RQ1.at[col], lsem.at[0])
    own_q.start()
    RC1[col] = CS[...]

    own_q.wait()
    drain(RQ1.at[pl.ds(0, 15)], q1r.at[0])
    drain(RC1.at[pl.ds(0, 15)], q1r.at[1])
    RQ2[zh, 0:8] = jnp.sum(RQ1[...], axis=0)
    RQ2[zh, 8:12] = jnp.sum(RC1[...], axis=0)
    for n in range(1, 4):
        device = (col * 4 + lax.rem(zh + n, 4), tt)
        remote(RQ2.at[zh], RQ2.at[zh], q2s, q2r, device).start()

    squares = jnp.zeros((16, 128), F32)

    def halves(ref, slot, at, squares):
        for part in range(4):
            chunk, f = part // 2, part % 2
            block = ref[slot, pl.ds(part, 16, stride=4), :]
            squares = squares + block * block
            high = block.astype(BF16)
            rows = slice(at + slot * 32 + chunk * 16, at + slot * 32 + chunk * 16 + 16)
            EH[rows, f * 128 : f * 128 + 128] = high
            EL[rows, f * 128 : f * 128 + 128] = (block - high.astype(F32)).astype(BF16)
        return squares

    for own in owns:
        own.wait()
    forwards = []
    for slot in range(8):
        drain(EO.at[slot, pl.ds(0, 60 if slot == 0 else 64)], er.at[slot])
        copy = remote(EO.at[slot], EP.at[slot], fs.at[slot], fr.at[slot], mate)
        copy.start()
        forwards.append(copy)
        squares = halves(EO, slot, 0, squares)
    for slot in range(8):
        forwards[slot].wait_recv()
        squares = halves(EP, slot, 256, squares)

    drain(RQ2.at[pl.ds(0, 3)], q2r)
    total = jnp.sum(RQ2[...], axis=0)
    queries = jnp.concatenate([total[0:4], total[4:8]], axis=1) / total[8:12, 0:1]

    def stacked(v):
        high = v.astype(BF16).astype(F32)
        return jnp.concatenate([high, v - high], axis=0).astype(BF16)

    def product(v, contract):
        v = stacked(v)
        dims = (((1,), (contract,)), ((), ()))
        whole = lax.dot_general(v, EH[...], dims, preferred_element_type=F32) + lax.dot_general(
            v, EL[...], dims, preferred_element_type=F32
        )
        return whole[0:4] + whole[4:8]

    spot = lax.broadcasted_iota(jnp.int32, (4, 128), 1)

    def share(step, partial_value, first, second):
        for b in range(4):
            RB[step, col, b] = partial_value[:, b * 128 : b * 128 + 128]
        RB[step, col, 4] = jnp.where(spot == 0, first, jnp.where(spot == 1, second, 0.0))

        def send(there, device):
            remote(RB.at[step, col], RB.at[step, col], rs.at[step], rr.at[step], device).start()

        plane(send)
        drain(RB.at[step, pl.ds(0, 15)], rr.at[step])
        whole = jnp.sum(RB[step], axis=0)
        return (
            jnp.concatenate([whole[b] for b in range(4)], axis=1),
            whole[4][:, 0:1],
            whole[4][:, 1:2],
        )

    def rowsum(v):
        return jnp.sum(v, axis=1, keepdims=True)

    residual = direction = queries
    trace = jnp.sum(jnp.sum(squares, axis=0, keepdims=True), axis=1, keepdims=True)
    seen, norm_now, trace = share(0, product(residual, 1), rowsum(residual * residual), trace)
    scale = TRAIN * (DAMP * (trace / TRAIN) / FEAT)
    length = norm_now
    scores = None
    for step in range(3):
        alpha = norm_now / (length + rowsum(seen * seen) / scale)
        scores = alpha * seen if step == 0 else scores + alpha * seen
        if step == 2:
            break
        image = direction + product(seen, 0) / scale
        residual = residual - alpha * image
        fresh_seen, fresh, along = share(
            step + 1, product(residual, 1), rowsum(residual * residual), rowsum(residual * direction)
        )
        beta = fresh / norm_now
        seen = fresh_seen + beta * seen
        length = fresh + 2.0 * beta * along + beta * beta * length
        direction = residual + beta * direction
        norm_now = fresh

    for h in range(2):
        SC[h] = scores[:, h * 256 : h * 256 + 128]
    for n, device in enumerate((mate, across, corner)):
        for p in range(2):
            remote(
                SC.at[lax.rem(p + k, 2)], FR.at[p, tt], osem.at[n], orem.at[n * 2 + p], device
            ).start()
    for p in range(2):
        FR[p, tt] = SC[lax.rem(p + k, 2)]
    for n in range(6):
        drain(FR.at[0, 0], orem.at[n])
    own = zl * 16 + col
    group = lax.broadcasted_iota(jnp.int32, (4, 4, 128), 0)
    place = jnp.where(group < 2, k * 64, (1 - k) * 32) + own
    place = lax.broadcasted_iota(jnp.int32, (4, 4, 128), 2) == place
    left = jnp.sum(jnp.where(place, FR[0], 0.0), axis=2, keepdims=True)
    right = jnp.sum(jnp.where(place, FR[1], 0.0), axis=2, keepdims=True)
    out[...] = jnp.where(lax.broadcasted_iota(jnp.int32, (4, 4, 2), 2) == 0, left, right)

    core_q.wait_send()
    cross_q.wait_send()
    for copy in core + cross + forwards:
        copy.wait_send()
    drain(RQ1.at[pl.ds(0, 15)], q1s.at[0])
    drain(RC1.at[pl.ds(0, 15)], q1s.at[1])
    drain(RQ2.at[pl.ds(0, 3)], q2s)
    for slot in range(8):
        drain(EO.at[slot, pl.ds(0, 60 if slot == 0 else 64)], es.at[slot])
    for step in range(3):
        drain(RB.at[step, pl.ds(0, 15)], rs.at[step])
    for n in range(3):
        drain(FR.at[0, pl.ds(0, 2)], osem.at[n])


def per_device(th, tg, tids, qh, qg, qids, pin, pout):
    V = pltpu.VMEM
    D = pltpu.SemaphoreType.DMA
    scores = pl.pallas_call(
        kernel,
        out_shape=jax.ShapeDtypeStruct((4, 4, 2), F32),
        in_specs=[pl.BlockSpec(memory_space=pl.ANY)] * 8,
        out_specs=pl.BlockSpec(memory_space=pltpu.VMEM),
        scratch_shapes=[
            V((4, 2) + th.shape[1:], BF16), V((4, 2) + tg.shape[1:], BF16), V(qh.shape, BF16), V(qg.shape, BF16),
            V(tids.shape, jnp.int32), V(qids.shape, jnp.int32),
            V((128, pin.shape[0]), BF16), V((128, pout.shape[0]), BF16),
            V((2, 2, 64, 128), F32), V((4, 2, 128, 128), F32),
            V((2, 64, 128), F32), V((4, 128, 128), F32),
            V((2, 64, 128), F32), V((4, 128, 128), F32),
            V((64, 128), F32), V((2, 128, 128), F32),
            V((128, 128), F32), V((16, 8, 128), F32),
            V((4, 128), F32), V((16, 4, 128), F32),
            V((4, 12, 128), F32),
            V((2, 32, 128), F32), V((8, 64, 128), F32), V((8, 64, 128), F32),
            V((512, 256), BF16), V((512, 256), BF16),
            V((3, 16, 5, 4, 128), F32),
            V((2, 4, 128), F32), V((2, 4, 4, 128), F32),
            D((14,)), D((5,)), D((5,)), D((3,)), D((3,)), D((2,)), D((2,)), D, D,
            D((8,)), D((8,)), D((8,)), D((8,)), D((3,)), D((3,)), D((3,)), D((6,)), D((3,)),
            pltpu.SemaphoreType.REGULAR,
        ],
        compiler_params=pltpu.CompilerParams(
            collective_id=0, has_side_effects=True, vmem_limit_bytes=56 * 1024 * 1024
        ),
        cost_estimate=pl.CostEstimate(flops=10**9, bytes_accessed=13 * 10**6, transcendentals=0),
    )(th, tg, tids, qh, qg, qids, pin.T, pout.T)
    return scores.reshape(16, 2)


def solution(mesh):
    return jax.shard_map(
        per_device,
        mesh=mesh,
        in_specs=(
            P("dp", None, "tensor"),
            P("dp", None, "tensor"),
            P("dp", None),
            P(None, "dp", "tensor"),
            P(None, "dp", "tensor"),
            P(None, "dp"),
            P("tensor", None),
            P("tensor", None),
        ),
        out_specs=P(None, ("dp", "tensor")),
        check_vma=False,
    )
```

time: 63.4 us -> 53.8 us (0.85)
  Pallas kernels: 57.9 us -> 52.3 us
  local copies, waits for them, and re-layouts: 5.32 us -> 1.33 us
    pallas_call x1, Pallas kernels: 57.9 us -> 52.3 us  [per_device(): pl.pallas_call(kernel, out_shape=jax.ShapeDtypeStruct((4, 4, 2), F32), in...]
    unnamed x2 -> x0, local copies, waits for them, and re-layouts: 3.99 us -> none
where the time goes in v2:
time: 53.8 us; the launch traced here: 53.7 us
  Pallas kernels  52.3 us (97%)
  local copies, waits for them, and re-layouts  1.33 us (2%)
    pallas_call x1, Pallas kernels, per_device(): pl.pallas_call(kernel, out_shape=jax.ShapeDtypeStruct((4, 4, 2), F32), in...  52.3 us
    reshape x1, local copies, waits for them, and re-layouts, per_device(): return scores.reshape(16, 2)  1.33 us

profile of v2, /device:TPU:1, one launch (start us, length us, event | category | flops | bytes accessed | tf_op | source)
XLA Modules:
  0.0 53.7 jit_solution(10009829460798350861)
XLA Ops:
  0.0 52.3 %shard_map.82 = f32[4,4,2]{2,1,0:T(4,128)} custom-call(bf16[8,128,3584]{2,1,0:T(8,128)(2,1)} %th.1, bf16[8,128,1024]{2,1,0:T(8,128)(2,1)} %tg.1, s32[8,128]{1,0:T(8,128)} %tids.1, bf16[16,16,3584]{2,1,0:T(8,128)(2,1)} %qh.1, bf16[16,16,1024]{2,1,0:T(8,128)(2,1)} %qg.1, s32[16,16]{1,0:T(8,128)} %qids.1, bf16[64,3584]{1,0:T(8,128)(2,1)} %bitcast.3, ...), custom_call_target="tpu_custom_call" | custom-call | flops 1000000000 | bytes 13000000 | tf_op jit(solution)/shard_map/pallas_call | solution.py:334
  52.3 1.3 %copy.10 = f32[16,2]{0,1:T(2,128)} copy(f32[16,2]{1,0:T(8,128)} %bitcast.5) | data formatting | bytes 256 | tf_op jit(solution)/shard_map/reshape | solution.py:363

commit v3 on v2

--- a/solution.py
+++ b/solution.py
@@ -21,7 +21,7 @@
     th, tg, tids, qh, qg, qids, pin, pout, out,
     TH, TG, QH, QG, TIDS, QIDS, WI, WO,
     XQ, XT, RCQ, RCT, YQ, YT, RZQ, RZT,
-    QPS, RQ1, CS, RC1, RQ2, ES, EO, EP, EH, EL, RB, SC, FR,
+    QPS, RQ1, CS, RC1, RQ2, ES, EO, EP, EH, EL, RB, SC, FR, OUT,
     hsem, cs, cr, zs, zr, q1s, q1r, q2s, q2r, es, er, fs, fr, rs, rr, osem, orem, lsem, inside,
 ):
     dp = lax.axis_index("dp")
@@ -55,6 +55,29 @@
         lax.fori_loop(0, 6, body, 0)
         lax.fori_loop(7, 16, body, 0)
 
+    def unit_loads(unit):
+        pair = pl.ds((unit % 2) * 4 + (far if unit < 2 else zl) * 2, 2)
+        return [
+            pltpu.make_async_copy(th.at[pair], TH.at[unit], hsem.at[6 + 2 * unit]),
+            pltpu.make_async_copy(tg.at[pair], TG.at[unit], hsem.at[7 + 2 * unit]),
+        ]
+
+    weights = [
+        pltpu.make_async_copy(pin, WI.at[0:64], hsem.at[0]),
+        pltpu.make_async_copy(pout, WO.at[64:128], hsem.at[1]),
+    ]
+    units = [unit_loads(unit) for unit in range(4)]
+    query = [
+        pltpu.make_async_copy(qh, QH, hsem.at[2]),
+        pltpu.make_async_copy(qg, QG, hsem.at[3]),
+    ]
+    ids = [
+        pltpu.make_async_copy(qids, QIDS, hsem.at[4]),
+        pltpu.make_async_copy(tids, TIDS, hsem.at[5]),
+    ]
+    for load in weights + units[0]:
+        load.start()
+
     barrier = pltpu.get_barrier_semaphore()
 
     def greet(device):
@@ -66,19 +89,7 @@
     greet(mate)
     greet(corner)
 
-    loads = [
-        pltpu.make_async_copy(pin, WI.at[0:64], hsem.at[0]),
-        pltpu.make_async_copy(qh, QH, hsem.at[1]),
-        pltpu.make_async_copy(pout, WO.at[64:128], hsem.at[2]),
-        pltpu.make_async_copy(qg, QG, hsem.at[3]),
-        pltpu.make_async_copy(qids, QIDS, hsem.at[4]),
-        pltpu.make_async_copy(tids, TIDS, hsem.at[5]),
-    ]
-    for unit in range(4):
-        pair = pl.ds((unit % 2) * 4 + (far if unit < 2 else zl) * 2, 2)
-        loads.append(pltpu.make_async_copy(th.at[pair], TH.at[unit], hsem.at[6 + 2 * unit]))
-        loads.append(pltpu.make_async_copy(tg.at[pair], TG.at[unit], hsem.at[7 + 2 * unit]))
-    for load in loads:
+    for load in units[1] + query + units[2] + units[3] + ids:
         load.start()
 
     def remote(src, dst, send, recv, device):
@@ -98,25 +109,34 @@
 
     WI[64:128] = jnp.zeros_like(WI[64:128])
     WO[0:64] = jnp.zeros_like(WO[0:64])
-    for n in range(4):
-        loads[n].wait()
+    def train_unit(unit):
+        for load in units[unit]:
+            load.wait()
+        for half in range(2):
+            XT[unit, half] = project(TH[unit, half], TG[unit, half])
+
+    for load in weights:
+        load.wait()
+    train_unit(0)
+    train_unit(1)
+    for load in query:
+        load.wait()
     for half in range(2):
         rows = slice(half * 8, half * 8 + 8)
         XQ[half] = project(QH[rows].reshape(128, -1), QG[rows].reshape(128, -1)).reshape(2, 64, 128)
-    for unit in range(4):
-        loads[6 + 2 * unit].wait()
-        loads[7 + 2 * unit].wait()
-        for half in range(2):
-            XT[unit, half] = project(TH[unit, half], TG[unit, half])
 
     pl.semaphore_wait(barrier, 24)
     core = [remote(XT.at[u, 1 - k], RCT.at[u], cs.at[u], cr.at[u], mate) for u in range(4)]
     core_q = remote(XQ.at[:, 1 - k], RCQ, cs.at[4], cr.at[4], mate)
-    for copy in core[:2] + [core_q] + core[2:]:
+    for copy in [core_q] + core[:2]:
         copy.start()
     for step in range(1, 8):
         pl.semaphore_signal(inside, inc=1, device_id=level(col, step), device_id_type=MESH)
 
+    core_q.wait_recv()
+    YQ[...] = XQ[:, k] + RCQ[...]
+    cross_q = remote(YQ.at[far], RZQ, zs.at[2], zr.at[2], across)
+    cross_q.start()
     cross = []
     for u in range(2):
         core[u].wait_recv()
@@ -124,57 +144,16 @@
         copy = remote(YT.at[u], RZT.at[u], zs.at[u], zr.at[u], across)
         copy.start()
         cross.append(copy)
-    core_q.wait_recv()
-    YQ[...] = XQ[:, k] + RCQ[...]
-    cross_q = remote(YQ.at[far], RZQ, zs.at[2], zr.at[2], across)
-    cross_q.start()
     for u in range(2, 4):
-        core[u].wait_recv()
-        YT[u] = XT[u, k] + RCT[u]
+        train_unit(u)
+        core[u].start()
 
     lane = lax.broadcasted_iota(jnp.int32, (32, 128), 1)
 
     def pack(both):
         return jnp.where(lane < 64, pltpu.roll(both[0:32], 64, 1), both[32:64])
 
-    def send_features(chunk, there, steps):
-        for step in steps:
-            slot = SLOT[step]
-            remote(
-                ES.at[chunk, pl.ds(there * 2, 2)], EO.at[slot, pl.ds(col * 4 + chunk * 2, 2)],
-                es.at[slot], er.at[slot], level(there, step),
-            ).start()
-
-    loads[5].wait()
-    owns = []
-    for chunk in range(2):
-        cross[chunk].wait_recv()
-        tokens = YT[2 + chunk] + RZT[chunk]
-        mask = (TIDS[pl.ds(chunk * 4 + tt, 1), :] != PAD_ID).astype(F32)
-        both = jnp.dot(
-            tokens.T[0:64] * mask, tokens,
-            precision=lax.Precision.HIGHEST, preferred_element_type=F32,
-        )
-        packed = pack(both) / jnp.sum(mask, axis=1, keepdims=True)
-        for f in range(2):
-            ES[chunk, pl.ds(f, 16, stride=2), :] = packed[f * 16 : f * 16 + 16]
-        if chunk == 0:
-            pl.semaphore_wait(inside, 7)
-
-        def features(n, carry, chunk=chunk):
-            send_features(chunk, column(n), (4, 5, 3, 6, 2, 7, 1, 0))
-            return carry
-
-        lax.fori_loop(0, 6, features, 0)
-        lax.fori_loop(7, 16, features, 0)
-        send_features(chunk, col, (4, 5, 3, 6, 2, 7, 1))
-        own = pltpu.make_async_copy(
-            ES.at[chunk, pl.ds(col * 2, 2)], EO.at[0, pl.ds(col * 4 + chunk * 2, 2)], lsem.at[1 + chunk]
-        )
-        own.start()
-        owns.append(own)
-
-    loads[4].wait()
+    ids[0].wait()
     cross_q.wait_recv()
     side = YQ[zl] + RZQ[...]
     mask = (QIDS[pl.ds(tt * 4, 4), :] != PAD_ID).astype(F32)
@@ -198,6 +177,44 @@
     own_q = pltpu.make_async_copy(QPS.at[pl.ds(col * 8, 8)], RQ1.at[col], lsem.at[0])
     own_q.start()
     RC1[col] = CS[...]
+
+    def send_features(chunk, there, steps):
+        for step in steps:
+            slot = SLOT[step]
+            remote(
+                ES.at[chunk, pl.ds(there * 2, 2)], EO.at[slot, pl.ds(col * 4 + chunk * 2, 2)],
+                es.at[slot], er.at[slot], level(there, step),
+            ).start()
+
+    ids[1].wait()
+    owns = []
+    for chunk in range(2):
+        core[2 + chunk].wait_recv()
+        cross[chunk].wait_recv()
+        tokens = XT[2 + chunk, k] + RCT[2 + chunk] + RZT[chunk]
+        mask = (TIDS[pl.ds(chunk * 4 + tt, 1), :] != PAD_ID).astype(F32)
+        both = jnp.dot(
+            tokens.T[0:64] * mask, tokens,
+            precision=lax.Precision.HIGHEST, preferred_element_type=F32,
+        )
+        packed = pack(both) / jnp.sum(mask, axis=1, keepdims=True)
+        for f in range(2):
+            ES[chunk, pl.ds(f, 16, stride=2), :] = packed[f * 16 : f * 16 + 16]
+        if chunk == 0:
+            pl.semaphore_wait(inside, 7)
+
+        def features(n, carry, chunk=chunk):
+            send_features(chunk, column(n), (4, 5, 3, 6, 2, 7, 1, 0))
+            return carry
+
+        lax.fori_loop(0, 6, features, 0)
+        lax.fori_loop(7, 16, features, 0)
+        send_features(chunk, col, (4, 5, 3, 6, 2, 7, 1))
+        own = pltpu.make_async_copy(
+            ES.at[chunk, pl.ds(col * 2, 2)], EO.at[0, pl.ds(col * 4 + chunk * 2, 2)], lsem.at[1 + chunk]
+        )
+        own.start()
+        owns.append(own)
 
     own_q.wait()
     drain(RQ1.at[pl.ds(0, 15)], q1r.at[0])
@@ -299,19 +316,30 @@
     for n, device in enumerate((mate, across, corner)):
         for p in range(2):
             remote(
-                SC.at[lax.rem(p + k, 2)], FR.at[p, tt], osem.at[n], orem.at[n * 2 + p], device
+                SC.at[lax.rem(p + k, 2)], FR.at[p, pl.ds(tt * 4, 4)], osem.at[n], orem.at[n * 2 + p], device
             ).start()
-    for p in range(2):
-        FR[p, tt] = SC[lax.rem(p + k, 2)]
+    mine = [
+        pltpu.make_async_copy(SC.at[lax.rem(p + k, 2)], FR.at[p, pl.ds(tt * 4, 4)], lsem.at[3 + p])
+        for p in range(2)
+    ]
+    for copy in mine:
+        copy.start()
+    group = lax.rem(lax.div(lax.broadcasted_iota(jnp.int32, (32, 128), 0), 4), 4)
+    place = jnp.where(group < 2, k * 64, (1 - k) * 32) + zl * 16 + col
+    place = lax.broadcasted_iota(jnp.int32, (32, 128), 1) == place
+    for copy in mine:
+        copy.wait()
     for n in range(6):
-        drain(FR.at[0, 0], orem.at[n])
-    own = zl * 16 + col
-    group = lax.broadcasted_iota(jnp.int32, (4, 4, 128), 0)
-    place = jnp.where(group < 2, k * 64, (1 - k) * 32) + own
-    place = lax.broadcasted_iota(jnp.int32, (4, 4, 128), 2) == place
-    left = jnp.sum(jnp.where(place, FR[0], 0.0), axis=2, keepdims=True)
-    right = jnp.sum(jnp.where(place, FR[1], 0.0), axis=2, keepdims=True)
-    out[...] = jnp.where(lax.broadcasted_iota(jnp.int32, (4, 4, 2), 2) == 0, left, right)
+        drain(FR.at[0, pl.ds(0, 4)], orem.at[n])
+    picked = jnp.where(place, FR[...].reshape(32, 128), 0.0)
+    turned = lax.dot_general(
+        jnp.ones((8, 128), F32), picked, (((1,), (1,)), ((), ())),
+        precision=lax.Precision.HIGHEST, preferred_element_type=F32,
+    )
+    OUT[0:1] = turned[0:1, 0:16]
+    OUT[1:2] = turned[0:1, 16:32]
+    result = pltpu.make_async_copy(OUT, out, lsem.at[5])
+    result.start()
 
     core_q.wait_send()
     cross_q.wait_send()
@@ -325,7 +353,8 @@
     for step in range(3):
         drain(RB.at[step, pl.ds(0, 15)], rs.at[step])
     for n in range(3):
-        drain(FR.at[0, pl.ds(0, 2)], osem.at[n])
+        drain(FR.at[0, pl.ds(0, 8)], osem.at[n])
+    result.wait()
 
 
 def per_device(th, tg, tids, qh, qg, qids, pin, pout):
@@ -333,16 +362,16 @@
     D = pltpu.SemaphoreType.DMA
     scores = pl.pallas_call(
         kernel,
-        out_shape=jax.ShapeDtypeStruct((4, 4, 2), F32),
+        out_shape=jax.ShapeDtypeStruct((2, 16), F32),
         in_specs=[pl.BlockSpec(memory_space=pl.ANY)] * 8,
-        out_specs=pl.BlockSpec(memory_space=pltpu.VMEM),
+        out_specs=pl.BlockSpec(memory_space=pl.ANY),
         scratch_shapes=[
             V((4, 2) + th.shape[1:], BF16), V((4, 2) + tg.shape[1:], BF16), V(qh.shape, BF16), V(qg.shape, BF16),
             V(tids.shape, jnp.int32), V(qids.shape, jnp.int32),
             V((128, pin.shape[0]), BF16), V((128, pout.shape[0]), BF16),
             V((2, 2, 64, 128), F32), V((4, 2, 128, 128), F32),
             V((2, 64, 128), F32), V((4, 128, 128), F32),
-            V((2, 64, 128), F32), V((4, 128, 128), F32),
+            V((2, 64, 128), F32), V((2, 128, 128), F32),
             V((64, 128), F32), V((2, 128, 128), F32),
             V((128, 128), F32), V((16, 8, 128), F32),
             V((4, 128), F32), V((16, 4, 128), F32),
@@ -350,9 +379,9 @@
             V((2, 32, 128), F32), V((8, 64, 128), F32), V((8, 64, 128), F32),
             V((512, 256), BF16), V((512, 256), BF16),
             V((3, 16, 5, 4, 128), F32),
-            V((2, 4, 128), F32), V((2, 4, 4, 128), F32),
+            V((2, 4, 128), F32), V((2, 16, 128), F32), V((2, 16), F32),
             D((14,)), D((5,)), D((5,)), D((3,)), D((3,)), D((2,)), D((2,)), D, D,
-            D((8,)), D((8,)), D((8,)), D((8,)), D((3,)), D((3,)), D((3,)), D((6,)), D((3,)),
+            D((8,)), D((8,)), D((8,)), D((8,)), D((3,)), D((3,)), D((3,)), D((6,)), D((6,)),
             pltpu.SemaphoreType.REGULAR,
         ],
         compiler_params=pltpu.CompilerParams(
@@ -360,7 +389,7 @@
         ),
         cost_estimate=pl.CostEstimate(flops=10**9, bytes_accessed=13 * 10**6, transcendentals=0),
     )(th, tg, tids, qh, qg, qids, pin.T, pout.T)
-    return scores.reshape(16, 2)
+    return scores.T
 
 
 def solution(mesh):

time: 53.8 us -> 51.9 us (0.965)
  Pallas kernels: 52.3 us -> 50.6 us
    pallas_call x1, Pallas kernels: 52.3 us -> 50.6 us  [per_device(): pl.pallas_call(kernel, out_shape=jax.ShapeDtypeStruct((2, 16), F32), in_s...]
    reshape x1 -> x0, local copies, waits for them, and re-layouts: 1.33 us -> none  [per_device(): return scores.reshape(16, 2)]
    unnamed x0 -> x1, local copies, waits for them, and re-layouts: none -> 1.24 us
where the time goes in v3:
time: 51.9 us; the launch traced here: 51.8 us
  Pallas kernels  50.6 us (97%)
  local copies, waits for them, and re-layouts  1.24 us (2%)
    pallas_call x1, Pallas kernels, per_device(): pl.pallas_call(kernel, out_shape=jax.ShapeDtypeStruct((2, 16), F32), in_s...  50.6 us
    unnamed x1, local copies, waits for them, and re-layouts  1.24 us

profile of v3, /device:TPU:1, one launch (start us, length us, event | category | flops | bytes accessed | tf_op | source)
XLA Modules:
  0.0 51.8 jit_solution(14592874593164402837)
XLA Ops:
  0.0 50.6 %shard_map.82 = f32[2,16]{1,0:T(2,128)} custom-call(bf16[8,128,3584]{2,1,0:T(8,128)(2,1)} %th.1, bf16[8,128,1024]{2,1,0:T(8,128)(2,1)} %tg.1, s32[8,128]{1,0:T(8,128)} %tids.1, bf16[16,16,3584]{2,1,0:T(8,128)(2,1)} %qh.1, bf16[16,16,1024]{2,1,0:T(8,128)(2,1)} %qg.1, s32[16,16]{1,0:T(8,128)} %qids.1, bf16[64,3584]{1,0:T(8,128)(2,1)} %bitcast.3, ...), custom_call_target="tpu_custom_call" | custom-call | flops 1000000000 | bytes 13000000 | tf_op jit(solution)/shard_map/pallas_call | solution.py:363
  50.6 1.2 %copy.10 = f32[16,2]{0,1:T(2,128)} copy(f32[16,2]{0,1:T(2,128)} %bitcast.5) | data formatting | bytes 256

commit v4 on v3

--- a/solution.py
+++ b/solution.py
@@ -21,7 +21,7 @@
     th, tg, tids, qh, qg, qids, pin, pout, out,
     TH, TG, QH, QG, TIDS, QIDS, WI, WO,
     XQ, XT, RCQ, RCT, YQ, YT, RZQ, RZT,
-    QPS, RQ1, CS, RC1, RQ2, ES, EO, EP, EH, EL, RB, SC, FR, OUT,
+    QPS, RQ1, RQ2, ES, EO, EP, EH, EL, RB, SC, FR,
     hsem, cs, cr, zs, zr, q1s, q1r, q2s, q2r, es, er, fs, fr, rs, rr, osem, orem, lsem, inside,
 ):
     dp = lax.axis_index("dp")
@@ -42,9 +42,11 @@
         m = lax.rem(n + 10, 16)
         return lax.rem(y + lax.div(m, 4), 4) * 4 + lax.rem(x + lax.rem(m, 4), 4)
 
+    floors = [lax.rem(z + step, 8) for step in range(8)]
+    floors = [(lax.div(nz, 2), lax.rem(nz, 2) * 2 + k) for nz in floors]
+
     def level(there, step):
-        nz = lax.rem(z + step, 8)
-        return (there * 4 + lax.div(nz, 2), lax.rem(nz, 2) * 2 + k)
+        return (there * 4 + floors[step][0], floors[step][1])
 
     def plane(fn):
         def body(n, carry):
@@ -75,7 +77,7 @@
         pltpu.make_async_copy(qids, QIDS, hsem.at[4]),
         pltpu.make_async_copy(tids, TIDS, hsem.at[5]),
     ]
-    for load in weights + units[0]:
+    for load in weights + query:
         load.start()
 
     barrier = pltpu.get_barrier_semaphore()
@@ -89,7 +91,7 @@
     greet(mate)
     greet(corner)
 
-    for load in units[1] + query + units[2] + units[3] + ids:
+    for load in units[0] + units[1] + units[2] + units[3] + ids:
         load.start()
 
     def remote(src, dst, send, recv, device):
@@ -115,11 +117,7 @@
         for half in range(2):
             XT[unit, half] = project(TH[unit, half], TG[unit, half])
 
-    for load in weights:
-        load.wait()
-    train_unit(0)
-    train_unit(1)
-    for load in query:
+    for load in weights + query:
         load.wait()
     for half in range(2):
         rows = slice(half * 8, half * 8 + 8)
@@ -127,26 +125,31 @@
 
     pl.semaphore_wait(barrier, 24)
     core = [remote(XT.at[u, 1 - k], RCT.at[u], cs.at[u], cr.at[u], mate) for u in range(4)]
+    cross = [remote(YT.at[u], RZT.at[u], zs.at[u], zr.at[u], across) for u in range(2)]
     core_q = remote(XQ.at[:, 1 - k], RCQ, cs.at[4], cr.at[4], mate)
-    for copy in [core_q] + core[:2]:
-        copy.start()
+    cross_q = remote(YQ.at[far], RZQ, zs.at[2], zr.at[2], across)
+    core_q.start()
     for step in range(1, 8):
         pl.semaphore_signal(inside, inc=1, device_id=level(col, step), device_id_type=MESH)
 
+    def pass_on(u):
+        core[u].wait_recv()
+        YT[u] = XT[u, k] + RCT[u]
+        cross[u].start()
+
+    train_unit(0)
+    core[0].start()
     core_q.wait_recv()
     YQ[...] = XQ[:, k] + RCQ[...]
-    cross_q = remote(YQ.at[far], RZQ, zs.at[2], zr.at[2], across)
     cross_q.start()
-    cross = []
-    for u in range(2):
-        core[u].wait_recv()
-        YT[u] = XT[u, k] + RCT[u]
-        copy = remote(YT.at[u], RZT.at[u], zs.at[u], zr.at[u], across)
-        copy.start()
-        cross.append(copy)
-    for u in range(2, 4):
-        train_unit(u)
-        core[u].start()
+    train_unit(1)
+    core[1].start()
+    pass_on(0)
+    train_unit(2)
+    core[2].start()
+    pass_on(1)
+    train_unit(3)
+    core[3].start()
 
     lane = lax.broadcasted_iota(jnp.int32, (32, 128), 1)
 
@@ -157,7 +160,7 @@
     cross_q.wait_recv()
     side = YQ[zl] + RZQ[...]
     mask = (QIDS[pl.ds(tt * 4, 4), :] != PAD_ID).astype(F32)
-    CS[...] = jnp.broadcast_to(jnp.sum(mask, axis=1, keepdims=True), (4, 128))
+    count = jnp.broadcast_to(jnp.sum(mask, axis=1, keepdims=True), (4, 128))
     wide = jnp.concatenate([mask] * 4, axis=1)
     owner = lax.div(lax.broadcasted_iota(jnp.int32, (4, 64), 1), 16)
     wide = jnp.where(owner == lax.broadcasted_iota(jnp.int32, (4, 64), 0), wide, 0.0)
@@ -167,16 +170,17 @@
     for q in range(4):
         packed = pack(both[q * 64 : q * 64 + 64])
         for f in range(2):
-            QPS[pl.ds(f * 4 + q, 16, stride=8), :] = packed[f * 16 : f * 16 + 16]
+            QPS[pl.ds(f * 4 + q, 16, stride=12), :] = packed[f * 16 : f * 16 + 16]
+
+    for c in range(16):
+        QPS[c * 12 + 8 : c * 12 + 12, :] = count
 
     def send_q1(there, device):
-        remote(QPS.at[pl.ds(there * 8, 8)], RQ1.at[col], q1s.at[0], q1r.at[0], device).start()
-        remote(CS, RC1.at[col], q1s.at[1], q1r.at[1], device).start()
+        remote(QPS.at[pl.ds(there * 12, 12)], RQ1.at[col], q1s, q1r, device).start()
 
     plane(send_q1)
-    own_q = pltpu.make_async_copy(QPS.at[pl.ds(col * 8, 8)], RQ1.at[col], lsem.at[0])
+    own_q = pltpu.make_async_copy(QPS.at[pl.ds(col * 12, 12)], RQ1.at[col], lsem.at[0])
     own_q.start()
-    RC1[col] = CS[...]
 
     def send_features(chunk, there, steps):
         for step in steps:
@@ -217,10 +221,8 @@
         owns.append(own)
 
     own_q.wait()
-    drain(RQ1.at[pl.ds(0, 15)], q1r.at[0])
-    drain(RC1.at[pl.ds(0, 15)], q1r.at[1])
-    RQ2[zh, 0:8] = jnp.sum(RQ1[...], axis=0)
-    RQ2[zh, 8:12] = jnp.sum(RC1[...], axis=0)
+    drain(RQ1.at[pl.ds(0, 15)], q1r)
+    RQ2[zh] = jnp.sum(RQ1[...], axis=0)
     for n in range(1, 4):
         device = (col * 4 + lax.rem(zh + n, 4), tt)
         remote(RQ2.at[zh], RQ2.at[zh], q2s, q2r, device).start()
@@ -336,17 +338,14 @@
         jnp.ones((8, 128), F32), picked, (((1,), (1,)), ((), ())),
         precision=lax.Precision.HIGHEST, preferred_element_type=F32,
     )
-    OUT[0:1] = turned[0:1, 0:16]
-    OUT[1:2] = turned[0:1, 16:32]
-    result = pltpu.make_async_copy(OUT, out, lsem.at[5])
-    result.start()
+    out[0:1] = turned[0:1, 0:16]
+    out[1:2] = turned[0:1, 16:32]
 
     core_q.wait_send()
     cross_q.wait_send()
     for copy in core + cross + forwards:
         copy.wait_send()
-    drain(RQ1.at[pl.ds(0, 15)], q1s.at[0])
-    drain(RC1.at[pl.ds(0, 15)], q1s.at[1])
+    drain(RQ1.at[pl.ds(0, 15)], q1s)
     drain(RQ2.at[pl.ds(0, 3)], q2s)
     for slot in range(8):
         drain(EO.at[slot, pl.ds(0, 60 if slot == 0 else 64)], es.at[slot])
@@ -354,7 +353,6 @@
         drain(RB.at[step, pl.ds(0, 15)], rs.at[step])
     for n in range(3):
         drain(FR.at[0, pl.ds(0, 8)], osem.at[n])
-    result.wait()
 
 
 def per_device(th, tg, tids, qh, qg, qids, pin, pout):
@@ -362,9 +360,9 @@
     D = pltpu.SemaphoreType.DMA
     scores = pl.pallas_call(
         kernel,
-        out_shape=jax.ShapeDtypeStruct((2, 16), F32),
+        out_shape=pltpu.VMEM((2, 16), F32),
         in_specs=[pl.BlockSpec(memory_space=pl.ANY)] * 8,
-        out_specs=pl.BlockSpec(memory_space=pl.ANY),
+        out_specs=pl.BlockSpec(memory_space=pltpu.VMEM),
         scratch_shapes=[
             V((4, 2) + th.shape[1:], BF16), V((4, 2) + tg.shape[1:], BF16), V(qh.shape, BF16), V(qg.shape, BF16),
             V(tids.shape, jnp.int32), V(qids.shape, jnp.int32),
@@ -373,15 +371,14 @@
             V((2, 64, 128), F32), V((4, 128, 128), F32),
             V((2, 64, 128), F32), V((2, 128, 128), F32),
             V((64, 128), F32), V((2, 128, 128), F32),
-            V((128, 128), F32), V((16, 8, 128), F32),
-            V((4, 128), F32), V((16, 4, 128), F32),
+            V((192, 128), F32), V((16, 12, 128), F32),
             V((4, 12, 128), F32),
             V((2, 32, 128), F32), V((8, 64, 128), F32), V((8, 64, 128), F32),
             V((512, 256), BF16), V((512, 256), BF16),
             V((3, 16, 5, 4, 128), F32),
-            V((2, 4, 128), F32), V((2, 16, 128), F32), V((2, 16), F32),
-            D((14,)), D((5,)), D((5,)), D((3,)), D((3,)), D((2,)), D((2,)), D, D,
-            D((8,)), D((8,)), D((8,)), D((8,)), D((3,)), D((3,)), D((3,)), D((6,)), D((6,)),
+            V((2, 4, 128), F32), V((2, 16, 128), F32),
+            D((14,)), D((5,)), D((5,)), D((3,)), D((3,)), D, D, D, D,
+            D((8,)), D((8,)), D((8,)), D((8,)), D((3,)), D((3,)), D((3,)), D((6,)), D((5,)),
             pltpu.SemaphoreType.REGULAR,
         ],
         compiler_params=pltpu.CompilerParams(

time: 51.9 us -> 49.7 us (0.958)
  Pallas kernels: 50.6 us -> 49.1 us
  local copies, waits for them, and re-layouts: 1.24 us -> 0.56 us
    pallas_call x1, Pallas kernels: 50.6 us -> 49.1 us  [per_device(): pl.pallas_call(kernel, out_shape=pltpu.VMEM((2, 16), F32), in_specs=[pl.B...]
    unnamed x1, local copies, waits for them, and re-layouts: 1.24 us -> 0.56 us
where the time goes in v4:
time: 49.7 us; the launch traced here: 49.6 us
  Pallas kernels  49.1 us (99%)
  local copies, waits for them, and re-layouts  0.56 us (1%)
    pallas_call x1, Pallas kernels, per_device(): pl.pallas_call(kernel, out_shape=pltpu.VMEM((2, 16), F32), in_specs=[pl.B...  49.1 us

profile of v4, /device:TPU:1, one launch (start us, length us, event | category | flops | bytes accessed | tf_op | source)
XLA Modules:
  0.0 49.6 jit_solution(10976506077107183364)
XLA Ops:
  0.0 49.1 %shard_map.82 = f32[2,16]{1,0:T(2,128)S(1)} custom-call(bf16[8,128,3584]{2,1,0:T(8,128)(2,1)} %th.1, bf16[8,128,1024]{2,1,0:T(8,128)(2,1)} %tg.1, s32[8,128]{1,0:T(8,128)} %tids.1, bf16[16,16,3584]{2,1,0:T(8,128)(2,1)} %qh.1, bf16[16,16,1024]{2,1,0:T(8,128)(2,1)} %qg.1, s32[16,16]{1,0:T(8,128)} %qids.1, bf16[64,3584]{1,0:T(8,128)(2,1)} %bitcast.4, ...), custom_call_target="tpu_custom_call" | custom-call | flops 1000000000 | bytes 13000000 | tf_op jit(solution)/shard_map/pallas_call | solution.py:361
  49.1 0.6 %copy.10 = f32[16,2]{0,1:T(2,128)} copy(f32[16,2]{0,1:T(2,128)S(1)} %bitcast.3) | data formatting | bytes 256

commit v5 on v4

--- a/solution.py
+++ b/solution.py
@@ -48,14 +48,11 @@
     def level(there, step):
         return (there * 4 + floors[step][0], floors[step][1])
 
+    columns = [column(n) for n in range(16) if n != 6]
+
     def plane(fn):
-        def body(n, carry):
-            there = column(n)
+        for there in columns:
             fn(there, (there * 4 + zh, tt))
-            return carry
-
-        lax.fori_loop(0, 6, body, 0)
-        lax.fori_loop(7, 16, body, 0)
 
     def unit_loads(unit):
         pair = pl.ds((unit % 2) * 4 + (far if unit < 2 else zl) * 2, 2)
@@ -124,9 +121,9 @@
         XQ[half] = project(QH[rows].reshape(128, -1), QG[rows].reshape(128, -1)).reshape(2, 64, 128)
 
     pl.semaphore_wait(barrier, 24)
-    core = [remote(XT.at[u, 1 - k], RCT.at[u], cs.at[u], cr.at[u], mate) for u in range(4)]
+    core = [remote(XT.at[u, 1 - k], RCT.at[u], cs.at[0], cr.at[u], mate) for u in range(4)]
     cross = [remote(YT.at[u], RZT.at[u], zs.at[u], zr.at[u], across) for u in range(2)]
-    core_q = remote(XQ.at[:, 1 - k], RCQ, cs.at[4], cr.at[4], mate)
+    core_q = remote(XQ.at[:, 1 - k], RCQ, cs.at[1], cr.at[4], mate)
     cross_q = remote(YQ.at[far], RZQ, zs.at[2], zr.at[2], across)
     core_q.start()
     for step in range(1, 8):
@@ -187,7 +184,7 @@
             slot = SLOT[step]
             remote(
                 ES.at[chunk, pl.ds(there * 2, 2)], EO.at[slot, pl.ds(col * 4 + chunk * 2, 2)],
-                es.at[slot], er.at[slot], level(there, step),
+                es, er.at[slot], level(there, step),
             ).start()
 
     ids[1].wait()
@@ -245,7 +242,7 @@
     forwards = []
     for slot in range(8):
         drain(EO.at[slot, pl.ds(0, 60 if slot == 0 else 64)], er.at[slot])
-        copy = remote(EO.at[slot], EP.at[slot], fs.at[slot], fr.at[slot], mate)
+        copy = remote(EO.at[slot], EP.at[slot], fs, fr.at[slot], mate)
         copy.start()
         forwards.append(copy)
         squares = halves(EO, slot, 0, squares)
@@ -277,7 +274,7 @@
         RB[step, col, 4] = jnp.where(spot == 0, first, jnp.where(spot == 1, second, 0.0))
 
         def send(there, device):
-            remote(RB.at[step, col], RB.at[step, col], rs.at[step], rr.at[step], device).start()
+            remote(RB.at[step, col], RB.at[step, col], rs, rr.at[step], device).start()
 
         plane(send)
         drain(RB.at[step, pl.ds(0, 15)], rr.at[step])
@@ -318,7 +315,7 @@
     for n, device in enumerate((mate, across, corner)):
         for p in range(2):
             remote(
-                SC.at[lax.rem(p + k, 2)], FR.at[p, pl.ds(tt * 4, 4)], osem.at[n], orem.at[n * 2 + p], device
+                SC.at[lax.rem(p + k, 2)], FR.at[p, pl.ds(tt * 4, 4)], osem, orem.at[n * 2 + p], device
             ).start()
     mine = [
         pltpu.make_async_copy(SC.at[lax.rem(p + k, 2)], FR.at[p, pl.ds(tt * 4, 4)], lsem.at[3 + p])
@@ -343,16 +340,15 @@
 
     core_q.wait_send()
     cross_q.wait_send()
-    for copy in core + cross + forwards:
+    for copy in cross:
         copy.wait_send()
+    drain(RCT, cs.at[0])
+    drain(EO, fs)
     drain(RQ1.at[pl.ds(0, 15)], q1s)
     drain(RQ2.at[pl.ds(0, 3)], q2s)
-    for slot in range(8):
-        drain(EO.at[slot, pl.ds(0, 60 if slot == 0 else 64)], es.at[slot])
-    for step in range(3):
-        drain(RB.at[step, pl.ds(0, 15)], rs.at[step])
-    for n in range(3):
-        drain(FR.at[0, pl.ds(0, 8)], osem.at[n])
+    drain(XT.at[:, 0, pl.ds(0, 127)], es)
+    drain(RB.at[:, pl.ds(0, 15)], rs)
+    drain(FR.at[:, pl.ds(0, 12)], osem)
 
 
 def per_device(th, tg, tids, qh, qg, qids, pin, pout):
@@ -377,8 +373,8 @@
             V((512, 256), BF16), V((512, 256), BF16),
             V((3, 16, 5, 4, 128), F32),
             V((2, 4, 128), F32), V((2, 16, 128), F32),
-            D((14,)), D((5,)), D((5,)), D((3,)), D((3,)), D, D, D, D,
-            D((8,)), D((8,)), D((8,)), D((8,)), D((3,)), D((3,)), D((3,)), D((6,)), D((5,)),
+            D((14,)), D((2,)), D((5,)), D((3,)), D((3,)), D, D, D, D,
+            D, D((8,)), D, D((8,)), D, D((3,)), D, D((6,)), D((5,)),
             pltpu.SemaphoreType.REGULAR,
         ],
         compiler_params=pltpu.CompilerParams(

time: 49.7 us -> 49.5 us (level)
  no operation moved by 1% of the time
where the time goes in v5:
time: 49.5 us; the launch traced here: 49.4 us
  Pallas kernels  48.8 us (99%)
  local copies, waits for them, and re-layouts  0.56 us (1%)
    pallas_call x1, Pallas kernels, per_device(): pl.pallas_call(kernel, out_shape=pltpu.VMEM((2, 16), F32), in_specs=[pl.B...  48.8 us

profile of v5, /device:TPU:1, one launch (start us, length us, event | category | flops | bytes accessed | tf_op | source)
XLA Modules:
  0.0 49.4 jit_solution(3524164820694155185)
XLA Ops:
  0.0 48.8 %shard_map.82 = f32[2,16]{1,0:T(2,128)S(1)} custom-call(bf16[8,128,3584]{2,1,0:T(8,128)(2,1)} %th.1, bf16[8,128,1024]{2,1,0:T(8,128)(2,1)} %tg.1, s32[8,128]{1,0:T(8,128)} %tids.1, bf16[16,16,3584]{2,1,0:T(8,128)(2,1)} %qh.1, bf16[16,16,1024]{2,1,0:T(8,128)(2,1)} %qg.1, s32[16,16]{1,0:T(8,128)} %qids.1, bf16[64,3584]{1,0:T(8,128)(2,1)} %bitcast.4, ...), custom_call_target="tpu_custom_call" | custom-call | flops 1000000000 | bytes 13000000 | tf_op jit(solution)/shard_map/pallas_call | solution.py:357
  48.8 0.6 %copy.10 = f32[16,2]{0,1:T(2,128)} copy(f32[16,2]{0,1:T(2,128)S(1)} %bitcast.3) | data formatting | bytes 256

commit v6 on v5

--- a/solution.py
+++ b/solution.py
@@ -261,9 +261,14 @@
     def product(v, contract):
         v = stacked(v)
         dims = (((1,), (contract,)), ((), ()))
-        whole = lax.dot_general(v, EH[...], dims, preferred_element_type=F32) + lax.dot_general(
-            v, EL[...], dims, preferred_element_type=F32
-        )
+        parts = []
+        for n in range(2):
+            at = (slice(n * 256, n * 256 + 256), slice(0, 256)) if contract else (slice(0, 512), slice(n * 128, n * 128 + 128))
+            parts.append(
+                lax.dot_general(v, EH[at], dims, preferred_element_type=F32)
+                + lax.dot_general(v, EL[at], dims, preferred_element_type=F32)
+            )
+        whole = jnp.concatenate(parts, axis=1)
         return whole[0:4] + whole[4:8]
 
     spot = lax.broadcasted_iota(jnp.int32, (4, 128), 1)

time: 49.5 us -> 49.3 us (level)
  no operation moved by 1% of the time
where the time goes in v6:
time: 49.3 us
  Pallas kernels  48.7 us (99%)
  local copies, waits for them, and re-layouts  0.56 us (1%)
    pallas_call x1, Pallas kernels, per_device(): pl.pallas_call(kernel, out_shape=pltpu.VMEM((2, 16), F32), in_specs=[pl.B...  48.7 us

profile of v6, /device:TPU:1, one launch (start us, length us, event | category | flops | bytes accessed | tf_op | source)
XLA Modules:
  0.0 49.3 jit_solution(14624722414299931758)
XLA Ops:
  0.0 48.7 %shard_map.82 = f32[2,16]{1,0:T(2,128)S(1)} custom-call(bf16[8,128,3584]{2,1,0:T(8,128)(2,1)} %th.1, bf16[8,128,1024]{2,1,0:T(8,128)(2,1)} %tg.1, s32[8,128]{1,0:T(8,128)} %tids.1, bf16[16,16,3584]{2,1,0:T(8,128)(2,1)} %qh.1, bf16[16,16,1024]{2,1,0:T(8,128)(2,1)} %qg.1, s32[16,16]{1,0:T(8,128)} %qids.1, bf16[64,3584]{1,0:T(8,128)(2,1)} %bitcast.4, ...), custom_call_target="tpu_custom_call" | custom-call | flops 1000000000 | bytes 13000000 | tf_op jit(solution)/shard_map/pallas_call | solution.py:362
  48.7 0.6 %copy.10 = f32[16,2]{0,1:T(2,128)} copy(f32[16,2]{0,1:T(2,128)S(1)} %bitcast.3) | data formatting | bytes 256
